TPU v7x, 128 devices: a whole 4x4x4 slice. The times are simulated.
128 devices in a mesh: seq: 8 (over y, z_hi), head: 16 (over x, z_lo, core).
Axes of the slice: x: 4, y: 4, z: 4 (z_hi: 2, z_lo: 2; z = z_hi * 2 + z_lo), core: 2. Of those that a mesh axis runs over, the one named last changes fastest.
Arguments:
- sequence_activity: bfloat16 [2, 4096, 4096], P(None, 'seq', 'head'), may hold values from -6 to 6
- lookup_mapping_tensor: bfloat16 [4096, 16, 768], P(None, 'head'), may hold values from -1 to 1, as said below
- stepsize_mapping_matrix: bfloat16 [4096, 16], P(None, 'head'), may hold values from -0.09375 to 0.09375
- logit_sharpness: float32 [16], P('head'), may hold values from 4 to 120
- adapter_gain_vector: float32 [16, 256], P('head'), may hold values from 0.1 to 1.9
- starting_inner_left_matrix: float32 [16, 256, 512], P('head'), may hold values from -0.375 to 0.375
- starting_inner_right_matrix: float32 [16, 512, 256], P('head'), may hold values from -0.25 to 0.25
- final_mixing_matrix: bfloat16 [16, 256, 4096], P('head'), may hold values from -0.09375 to 0.09375
Outputs:
- mixed: bfloat16 [2, 4096, 4096], P(None, 'seq', 'head')
Inputs may be any that keep to these rules, and one draw needn't show every extreme that they name: `lookup_mapping_tensor`: entries of order 1 / sqrt(4096).
All inputs are finite; a program needn't handle non-finite values.
Results may differ from a plain program's by a relative error of at most 0.02.
Values may be sent and summed in bfloat16 or wider, within the bound.
A program may use at most 64 MiB of HBM per device.

v0:
```python
import jax
import jax.numpy as jnp
from jax import lax
from jax.sharding import PartitionSpec as P

WIN = 2048
NS_STEPS = 3
update_rate = 0.3


def shifted(block, axis, distance):
    devices = range(lax.axis_size(axis))
    route = [(i - distance, i) for i in devices if i - distance in devices]
    return lax.ppermute(block, axis, route)


def orthogonalize(update):
    scale = lax.rsqrt(jnp.sum(update * update) + 1e-06)
    current = update * scale
    for sweep in range(NS_STEPS):
        if current.shape[0] <= current.shape[1]:
            gram = jnp.dot(current, current.T, precision=lax.Precision.HIGHEST)
            current = 1.5 * current - 0.5 * jnp.dot(gram, current, precision=lax.Precision.HIGHEST)
        else:
            gram = jnp.dot(current.T, current, precision=lax.Precision.HIGHEST)
            current = 1.5 * current - 0.5 * jnp.dot(current, gram, precision=lax.Precision.HIGHEST)
    return current


def fast_group(weight_in, weight_out, keys, weighted, query_rows):
    in_half = weight_in.astype(jnp.bfloat16)
    out_half = weight_out.astype(jnp.bfloat16)
    hidden = jnp.dot(keys, in_half, preferred_element_type=jnp.float32)
    gating = jax.nn.sigmoid(hidden)
    activated = (hidden * gating).astype(jnp.bfloat16)
    grad_out = jnp.dot(activated.T, weighted, preferred_element_type=jnp.float32)
    backward = jnp.dot(weighted, out_half.T, preferred_element_type=jnp.float32)
    slopes = (backward * gating * (1.0 + hidden * (1.0 - gating))).astype(jnp.bfloat16)
    grad_in = jnp.dot(keys.T, slopes, preferred_element_type=jnp.float32)
    new_in = weight_in + update_rate * orthogonalize(grad_in)
    new_out = weight_out + update_rate * orthogonalize(grad_out)
    query_hidden = jnp.dot(
        query_rows, new_in.astype(jnp.bfloat16), preferred_element_type=jnp.float32
    )
    query_act = jax.nn.silu(query_hidden).astype(jnp.bfloat16)
    fast = jnp.dot(query_act, new_out.astype(jnp.bfloat16), preferred_element_type=jnp.float32)
    return (new_in, new_out, fast)


def prepare(projected, rate_col, count_seqs):
    head_dim = projected.shape[1] // 3
    query_rows = projected[:, :head_dim]
    keys = projected[:, head_dim : 2 * head_dim]
    values = projected[:, 2 * head_dim :]
    query_norm = (
        query_rows * lax.rsqrt(jnp.sum(query_rows * query_rows, axis=1, keepdims=True) + 1e-06)
    ).astype(jnp.bfloat16)
    key_norm = (keys * lax.rsqrt(jnp.sum(keys * keys, axis=1, keepdims=True) + 1e-06)).astype(
        jnp.bfloat16
    )
    value_half = values.astype(jnp.bfloat16)
    weighted = (jax.nn.softplus(rate_col) * values).astype(jnp.bfloat16)
    return (
        query_norm.reshape(count_seqs, -1, head_dim),
        key_norm.reshape(count_seqs, -1, head_dim),
        value_half.reshape(count_seqs, -1, head_dim),
        weighted.reshape(count_seqs, -1, head_dim),
    )


def attend_window(query_rows, keys, values, scale, start):
    count = query_rows.shape[1]
    window = keys.shape[1] - count
    scores = scale * jnp.einsum(
        "sqd,skd->sqk", query_rows, keys, preferred_element_type=jnp.float32
    )
    row_pos = lax.broadcasted_iota(jnp.int32, (count, count + window), 0)
    col_pos = lax.broadcasted_iota(jnp.int32, (count, count + window), 1)
    valid = (col_pos >= row_pos) & (col_pos <= row_pos + window) & (col_pos + start >= window)
    scores = jnp.where(valid[None], scores, -1e30)
    highest = jnp.max(scores, axis=2, keepdims=True)
    weights = jnp.exp(scores - highest)
    probs = (weights / jnp.sum(weights, axis=2, keepdims=True)).astype(jnp.bfloat16)
    return jnp.einsum("sqk,skd->sqd", probs, values, preferred_element_type=jnp.float32)


def combine(attended_output, fast, gain):
    normed = fast * lax.rsqrt(jnp.mean(fast * fast, axis=-1, keepdims=True) + 1e-05) * gain
    return (attended_output + normed).astype(jnp.bfloat16)


def body(
    sequence_activity,
    lookup_mapping_tensor,
    stepsize_mapping_matrix,
    logit_sharpness,
    adapter_gain_vector,
    starting_inner_left_matrix,
    starting_inner_right_matrix,
    final_mixing_matrix,
):
    seqs, head_group, local_width = sequence_activity.shape
    total_rows = seqs * head_group
    flattened = sequence_activity.reshape(total_rows, local_width)
    weights_in = lookup_mapping_tensor.reshape(
        lookup_mapping_tensor.shape[0], lookup_mapping_tensor.shape[2]
    )
    head_dim = weights_in.shape[1] // 3
    piece = lax.all_gather(flattened, "head", axis=1, tiled=True)
    projected = jnp.dot(piece, weights_in, preferred_element_type=jnp.float32)
    rate_col = jnp.dot(piece, stepsize_mapping_matrix, preferred_element_type=jnp.float32)
    query_rows, keys, values, weighted = prepare(projected, rate_col, seqs)
    token_position = lax.axis_index("seq")
    length = lax.axis_size("seq")
    reach = WIN // head_group
    hops = min(reach, length - 1)
    earlier = []
    current = (keys, values)
    for distance in range(hops):
        current = shifted((current[0], current[1]), "seq", 1)
        earlier.insert(0, current)
    windowed_key_rows = jnp.concatenate([pair[0] for pair in earlier] + [keys], axis=1)
    windowed_value_rows = jnp.concatenate([pair[1] for pair in earlier] + [values], axis=1)
    attended_output = attend_window(
        query_rows,
        windowed_key_rows,
        windowed_value_rows,
        logit_sharpness[0],
        token_position * head_group,
    )
    start_in = starting_inner_left_matrix[0]
    start_out = starting_inner_right_matrix[0]

    def turn(step, carry):
        held_in, held_out, fast_all = carry
        which = step // length
        live = step % length == token_position
        which = jnp.clip(which, 0, seqs - 1)
        use_in = jnp.where(token_position == 0, start_in, held_in)
        use_out = jnp.where(token_position == 0, start_out, held_out)
        block_keys = lax.dynamic_index_in_dim(keys, which, 0, keepdims=False)
        block_weighted = lax.dynamic_index_in_dim(weighted, which, 0, keepdims=False)
        block_queries = lax.dynamic_index_in_dim(query_rows, which, 0, keepdims=False)

        def working():
            return fast_group(use_in, use_out, block_keys, block_weighted, block_queries)

        def resting():
            return (use_in, use_out, jnp.zeros((head_group, head_dim), jnp.float32))

        new_in, new_out, fast = lax.cond(live, working, resting)
        stored = lax.dynamic_update_index_in_dim(fast_all, fast, which, 0)
        fast_all = jnp.where(live, stored, fast_all)
        sent_in, sent_out = shifted((new_in, new_out), "seq", 1)
        return (sent_in, sent_out, fast_all)

    turns = seqs * length
    carried = (start_in, start_out, jnp.zeros((seqs, head_group, head_dim), jnp.float32))
    carried = lax.fori_loop(0, turns, turn, carried)
    head_out = combine(attended_output, carried[2], adapter_gain_vector[0]).reshape(
        total_rows, head_dim
    )
    partial_value = jnp.dot(head_out, final_mixing_matrix[0], preferred_element_type=jnp.float32)
    result = lax.psum_scatter(
        partial_value.astype(jnp.bfloat16), "head", scatter_dimension=1, tiled=True
    )
    return result.reshape(seqs, head_group, -1)


def solution(mesh):
    in_specs = (
        P(None, "seq", "head"),
        P(None, "head", None),
        P(None, "head"),
        P("head"),
        P("head", None),
        P("head", None, None),
        P("head", None, None),
        P("head", None, None),
    )
    out_specs = P(None, "seq", "head")
    return jax.shard_map(body, mesh=mesh, in_specs=in_specs, out_specs=out_specs, check_vma=False)
```

profile of v0, /device:TPU:5, one launch (start us, length us, event | category | flops | bytes accessed | tf_op | source)
XLA Modules:
  0.0 1019.2 jit_solution(2209123766878446001)
XLA Ops:
  7.3 64.4 %all-gather.2.cloned.1.call-done = bf16[1024,4096]{1,0:T(8,128)(2,1)} async-done(((bf16[1024,256]{1,0:T(8,128)(2,1)}), bf16[1024,4096]{1,0:T(8,128)(2,1)}) %all-gather.2.cloned.1.call-update) | async-done | bytes 8388624 | tf_op jit(solution)/shard_map/all_gather | solution.py:109
  77.5 9.0 fusion.61
  154.4 659.3 %while.19 = (s32[]{:T(128)}, f32[256,512]{1,0:T(8,128)}, f32[512,256]{1,0:T(8,128)}, f32[2,512,256]{2,1,0:T(8,128)}, s32[]{:T(128)}, /*index=5*/pred[]{:T(512)},...) while((s32[]{:T(128)}, f32[256,512]{1,0:T(8,128)}, ...), condition=%wide.region_9.10_spmd, body=%wide.region_4.9_spmd.sunk | while | flops 5647237120 | bytes 32771644 | solution.py:159
  156.6 24.5 %conditional.2 = (f32[256,512]{1,0:T(8,128)S(1)}, f32[512,256]{1,0:T(8,128)S(1)}, f32[1,512,256]{2,1,0:T(8,128)}) conditional(s32[]{:T(128)} %convert_element_type.110, (f32[256,512]{1,0:T(8,128)S(1)}, f32[512,256]{1,0:T(8,128)S(1)}) %tuple.60, (bf16[2,512,256]{2,1,0:T(8,128)(2,1)}, s32[]{:T(128)}, bf16[2,512,256]{2,1,0:T(8,128)(2,1)}, ...), branch_computations={%region_5.5_spmd, %region_6.8_spmd} | conditional | flops 5646843904 | bytes 23857780 | solution.py:151
  192.0 11.2 %collective-permute-done.1 = f32[512,256]{1,0:T(8,128)} collective-permute-done((f32[512,256]{1,0:T(8,128)S(1)}, f32[512,256]{1,0:T(8,128)}, u32[]{:S(2)}, u32[]{:S(2)}) %collective-permute-start.1) | collective-permute-done | bytes 524320 | tf_op jit(solution)/shard_map/while/body/eval_jaxpr/ppermute | solution.py:14
  206.4 30.1 %collective-permute-start = (f32[256,512]{1,0:T(8,128)S(1)}, f32[256,512]{1,0:T(8,128)}, u32[]{:S(2)}, u32[]{:S(2)}) collective-permute-start(f32[256,512]{1,0:T(8,128)S(1)} %get-tuple-element.431), channel_id=1, source_target_pairs={{0,16},{16,32},{32,48},{48,64},{64,80},{80,96},{96,112},{1,17},{17... | collective-permute-start | bytes 1572872 | tf_op jit(solution)/shard_map/while/body/eval_jaxpr/ppermute | solution.py:14
  244.3 11.2 %collective-permute-done.1 = f32[512,256]{1,0:T(8,128)} collective-permute-done((f32[512,256]{1,0:T(8,128)S(1)}, f32[512,256]{1,0:T(8,128)}, u32[]{:S(2)}, u32[]{:S(2)}) %collective-permute-start.1) | collective-permute-done | bytes 524320 | tf_op jit(solution)/shard_map/while/body/eval_jaxpr/ppermute | solution.py:14
  265.2 26.7 %collective-permute-start.1 = (f32[512,256]{1,0:T(8,128)S(1)}, f32[512,256]{1,0:T(8,128)}, u32[]{:S(2)}, u32[]{:S(2)}) collective-permute-start(f32[512,256]{1,0:T(8,128)S(1)} %get-tuple-element.432), channel_id=1, source_target_pairs={{0,16},{16,32},{32,48},{48,64},{64,80},{80,96},{96,112},{1,17},{17... | collective-permute-start | bytes 1572872 | tf_op jit(solution)/shard_map/while/body/eval_jaxpr/ppermute | solution.py:14
  301.9 12.3 %collective-permute-start = (f32[256,512]{1,0:T(8,128)S(1)}, f32[256,512]{1,0:T(8,128)}, u32[]{:S(2)}, u32[]{:S(2)}) collective-permute-start(f32[256,512]{1,0:T(8,128)S(1)} %get-tuple-element.431), channel_id=1, source_target_pairs={{0,16},{16,32},{32,48},{48,64},{64,80},{80,96},{96,112},{1,17},{17... | collective-permute-start | bytes 1572872 | tf_op jit(solution)/shard_map/while/body/eval_jaxpr/ppermute | solution.py:14
  322.8 9.1 collective-permute-done.1
  335.0 20.9 %collective-permute-start = (f32[256,512]{1,0:T(8,128)S(1)}, f32[256,512]{1,0:T(8,128)}, u32[]{:S(2)}, u32[]{:S(2)}) collective-permute-start(f32[256,512]{1,0:T(8,128)S(1)} %get-tuple-element.431), channel_id=1, source_target_pairs={{0,16},{16,32},{32,48},{48,64},{64,80},{80,96},{96,112},{1,17},{17... | collective-permute-start | bytes 1572872 | tf_op jit(solution)/shard_map/while/body/eval_jaxpr/ppermute | solution.py:14
  355.9 11.5 %collective-permute-start.1 = (f32[512,256]{1,0:T(8,128)S(1)}, f32[512,256]{1,0:T(8,128)}, u32[]{:S(2)}, u32[]{:S(2)}) collective-permute-start(f32[512,256]{1,0:T(8,128)S(1)} %get-tuple-element.432), channel_id=1, source_target_pairs={{0,16},{16,32},{32,48},{48,64},{64,80},{80,96},{96,112},{1,17},{17... | collective-permute-start | bytes 1572872 | tf_op jit(solution)/shard_map/while/body/eval_jaxpr/ppermute | solution.py:14
  375.9 12.2 %collective-permute-start = (f32[256,512]{1,0:T(8,128)S(1)}, f32[256,512]{1,0:T(8,128)}, u32[]{:S(2)}, u32[]{:S(2)}) collective-permute-start(f32[256,512]{1,0:T(8,128)S(1)} %get-tuple-element.431), channel_id=1, source_target_pairs={{0,16},{16,32},{32,48},{48,64},{64,80},{80,96},{96,112},{1,17},{17... | collective-permute-start | bytes 1572872 | tf_op jit(solution)/shard_map/while/body/eval_jaxpr/ppermute | solution.py:14
  388.1 21.2 %collective-permute-start.1 = (f32[512,256]{1,0:T(8,128)S(1)}, f32[512,256]{1,0:T(8,128)}, u32[]{:S(2)}, u32[]{:S(2)}) collective-permute-start(f32[512,256]{1,0:T(8,128)S(1)} %get-tuple-element.432), channel_id=1, source_target_pairs={{0,16},{16,32},{32,48},{48,64},{64,80},{80,96},{96,112},{1,17},{17... | collective-permute-start | bytes 1572872 | tf_op jit(solution)/shard_map/while/body/eval_jaxpr/ppermute | solution.py:14
  417.9 12.6 %collective-permute-start = (f32[256,512]{1,0:T(8,128)S(1)}, f32[256,512]{1,0:T(8,128)}, u32[]{:S(2)}, u32[]{:S(2)}) collective-permute-start(f32[256,512]{1,0:T(8,128)S(1)} %get-tuple-element.431), channel_id=1, source_target_pairs={{0,16},{16,32},{32,48},{48,64},{64,80},{80,96},{96,112},{1,17},{17... | collective-permute-start | bytes 1572872 | tf_op jit(solution)/shard_map/while/body/eval_jaxpr/ppermute | solution.py:14
  430.5 11.8 %collective-permute-start.1 = (f32[512,256]{1,0:T(8,128)S(1)}, f32[512,256]{1,0:T(8,128)}, u32[]{:S(2)}, u32[]{:S(2)}) collective-permute-start(f32[512,256]{1,0:T(8,128)S(1)} %get-tuple-element.432), channel_id=1, source_target_pairs={{0,16},{16,32},{32,48},{48,64},{64,80},{80,96},{96,112},{1,17},{17... | collective-permute-start | bytes 1572872 | tf_op jit(solution)/shard_map/while/body/eval_jaxpr/ppermute | solution.py:14
  451.4 19.6 %collective-permute-start = (f32[256,512]{1,0:T(8,128)S(1)}, f32[256,512]{1,0:T(8,128)}, u32[]{:S(2)}, u32[]{:S(2)}) collective-permute-start(f32[256,512]{1,0:T(8,128)S(1)} %get-tuple-element.431), channel_id=1, source_target_pairs={{0,16},{16,32},{32,48},{48,64},{64,80},{80,96},{96,112},{1,17},{17... | collective-permute-start | bytes 1572872 | tf_op jit(solution)/shard_map/while/body/eval_jaxpr/ppermute | solution.py:14
  471.0 12.4 %collective-permute-start.1 = (f32[512,256]{1,0:T(8,128)S(1)}, f32[512,256]{1,0:T(8,128)}, u32[]{:S(2)}, u32[]{:S(2)}) collective-permute-start(f32[512,256]{1,0:T(8,128)S(1)} %get-tuple-element.432), channel_id=1, source_target_pairs={{0,16},{16,32},{32,48},{48,64},{64,80},{80,96},{96,112},{1,17},{17... | collective-permute-start | bytes 1572872 | tf_op jit(solution)/shard_map/while/body/eval_jaxpr/ppermute | solution.py:14
  492.1 24.5 %conditional.2 = (f32[256,512]{1,0:T(8,128)S(1)}, f32[512,256]{1,0:T(8,128)S(1)}, f32[1,512,256]{2,1,0:T(8,128)}) conditional(s32[]{:T(128)} %convert_element_type.110, (f32[256,512]{1,0:T(8,128)S(1)}, f32[512,256]{1,0:T(8,128)S(1)}) %tuple.60, (bf16[2,512,256]{2,1,0:T(8,128)(2,1)}, s32[]{:T(128)}, bf16[2,512,256]{2,1,0:T(8,128)(2,1)}, ...), branch_computations={%region_5.5_spmd, %region_6.8_spmd} | conditional | flops 5646843904 | bytes 23857780 | solution.py:151
  525.9 8.8 collective-permute-done.1
  537.8 33.1 %collective-permute-start = (f32[256,512]{1,0:T(8,128)S(1)}, f32[256,512]{1,0:T(8,128)}, u32[]{:S(2)}, u32[]{:S(2)}) collective-permute-start(f32[256,512]{1,0:T(8,128)S(1)} %get-tuple-element.431), channel_id=1, source_target_pairs={{0,16},{16,32},{32,48},{48,64},{64,80},{80,96},{96,112},{1,17},{17... | collective-permute-start | bytes 1572872 | tf_op jit(solution)/shard_map/while/body/eval_jaxpr/ppermute | solution.py:14
  576.2 10.3 %collective-permute-done.1 = f32[512,256]{1,0:T(8,128)} collective-permute-done((f32[512,256]{1,0:T(8,128)S(1)}, f32[512,256]{1,0:T(8,128)}, u32[]{:S(2)}, u32[]{:S(2)}) %collective-permute-start.1) | collective-permute-done | bytes 524320 | tf_op jit(solution)/shard_map/while/body/eval_jaxpr/ppermute | solution.py:14
  596.2 26.8 %collective-permute-start.1 = (f32[512,256]{1,0:T(8,128)S(1)}, f32[512,256]{1,0:T(8,128)}, u32[]{:S(2)}, u32[]{:S(2)}) collective-permute-start(f32[512,256]{1,0:T(8,128)S(1)} %get-tuple-element.432), channel_id=1, source_target_pairs={{0,16},{16,32},{32,48},{48,64},{64,80},{80,96},{96,112},{1,17},{17... | collective-permute-start | bytes 1572872 | tf_op jit(solution)/shard_map/while/body/eval_jaxpr/ppermute | solution.py:14
  631.5 10.5 %collective-permute-start = (f32[256,512]{1,0:T(8,128)S(1)}, f32[256,512]{1,0:T(8,128)}, u32[]{:S(2)}, u32[]{:S(2)}) collective-permute-start(f32[256,512]{1,0:T(8,128)S(1)} %get-tuple-element.431), channel_id=1, source_target_pairs={{0,16},{16,32},{32,48},{48,64},{64,80},{80,96},{96,112},{1,17},{17... | collective-permute-start | bytes 1572872 | tf_op jit(solution)/shard_map/while/body/eval_jaxpr/ppermute | solution.py:14
  661.3 21.5 %collective-permute-start = (f32[256,512]{1,0:T(8,128)S(1)}, f32[256,512]{1,0:T(8,128)}, u32[]{:S(2)}, u32[]{:S(2)}) collective-permute-start(f32[256,512]{1,0:T(8,128)S(1)} %get-tuple-element.431), channel_id=1, source_target_pairs={{0,16},{16,32},{32,48},{48,64},{64,80},{80,96},{96,112},{1,17},{17... | collective-permute-start | bytes 1572872 | tf_op jit(solution)/shard_map/while/body/eval_jaxpr/ppermute | solution.py:14
  682.8 9.1 collective-permute-start.1
  693.8 9.0 collective-permute-done.1
  712.5 21.1 %collective-permute-start.1 = (f32[512,256]{1,0:T(8,128)S(1)}, f32[512,256]{1,0:T(8,128)}, u32[]{:S(2)}, u32[]{:S(2)}) collective-permute-start(f32[512,256]{1,0:T(8,128)S(1)} %get-tuple-element.432), channel_id=1, source_target_pairs={{0,16},{16,32},{32,48},{48,64},{64,80},{80,96},{96,112},{1,17},{17... | collective-permute-start | bytes 1572872 | tf_op jit(solution)/shard_map/while/body/eval_jaxpr/ppermute | solution.py:14
  742.1 13.7 %collective-permute-start = (f32[256,512]{1,0:T(8,128)S(1)}, f32[256,512]{1,0:T(8,128)}, u32[]{:S(2)}, u32[]{:S(2)}) collective-permute-start(f32[256,512]{1,0:T(8,128)S(1)} %get-tuple-element.431), channel_id=1, source_target_pairs={{0,16},{16,32},{32,48},{48,64},{64,80},{80,96},{96,112},{1,17},{17... | collective-permute-start | bytes 1572872 | tf_op jit(solution)/shard_map/while/body/eval_jaxpr/ppermute | solution.py:14
  775.7 16.5 %collective-permute-start = (f32[256,512]{1,0:T(8,128)S(1)}, f32[256,512]{1,0:T(8,128)}, u32[]{:S(2)}, u32[]{:S(2)}) collective-permute-start(f32[256,512]{1,0:T(8,128)S(1)} %get-tuple-element.431), channel_id=1, source_target_pairs={{0,16},{16,32},{32,48},{48,64},{64,80},{80,96},{96,112},{1,17},{17... | collective-permute-start | bytes 1572872 | tf_op jit(solution)/shard_map/while/body/eval_jaxpr/ppermute | solution.py:14
  792.1 11.0 %collective-permute-start.1 = (f32[512,256]{1,0:T(8,128)S(1)}, f32[512,256]{1,0:T(8,128)}, u32[]{:S(2)}, u32[]{:S(2)}) collective-permute-start(f32[512,256]{1,0:T(8,128)S(1)} %get-tuple-element.432), channel_id=1, source_target_pairs={{0,16},{16,32},{32,48},{48,64},{64,80},{80,96},{96,112},{1,17},{17... | collective-permute-start | bytes 1572872 | tf_op jit(solution)/shard_map/while/body/eval_jaxpr/ppermute | solution.py:14
  853.3 159.1 %reduce-scatter.2.cloned.1.call-done = bf16[1024,256]{1,0:T(8,128)(2,1)} async-done(((bf16[1024,4096]{1,0:T(8,128)(2,1)}), bf16[1024,256]{1,0:T(8,128)(2,1)}) %reduce-scatter.2.cloned.1.call-update) | async-done | bytes 524304 | tf_op jit(solution)/shard_map/reduce_scatter | solution.py:164
  (221 shorter events, 367.4 us)
Async XLA Ops:
  6.5 65.2 %all-gather.2.cloned.1.call-start = ((), (), s32[]{:S(2)}) async-start(), calls=%async_computation.1 | async-start | bytes 8912896 | tf_op jit(solution)/shard_map/all_gather | solution.py:109
  7.3 1005.1 %reduce-scatter.2.cloned.1.call-start = ((), (), s32[]{:S(2)}) async-start(), calls=%async_computation.2 | async-start | bytes 8912896 | tf_op jit(solution)/shard_map/reduce_scatter | solution.py:164
  92.8 20.4 %collective-permute-start.2 = (bf16[2,512,256]{2,1,0:T(8,128)(2,1)}, bf16[2,512,256]{2,1,0:T(8,128)(2,1)S(1)}, u32[]{:S(2)}, u32[]{:S(2)}) collective-permute-start(bf16[2,512,256]{2,1,0:T(8,128)(2,1)} %bitcast.8), channel_id=1, source_target_pairs={{0,16},{16,32},{32,48},{48,64},{64,80},{80,96},{96,112},{1,17},{17... | collective-permute-start | bytes 1572872 | tf_op jit(solution)/shard_map/ppermute | solution.py:14
  101.9 22.5 %collective-permute-start.7 = (bf16[2,512,256]{2,1,0:T(8,128)(2,1)S(1)}, bf16[2,512,256]{2,1,0:T(8,128)(2,1)}, u32[]{:S(2)}, u32[]{:S(2)}) collective-permute-start(bf16[2,512,256]{2,1,0:T(8,128)(2,1)S(1)} %collective-permute-done.6), channel_id=1, source_target_pairs={{0,16},{16,32},{32,48},{48,64},{64,80},{80,96},{96,112},{1,17},{17... | collective-permute-start | bytes 1572872 | tf_op jit(solution)/shard_map/ppermute | solution.py:14
  113.2 22.4 %collective-permute-start.3 = (bf16[2,512,256]{2,1,0:T(8,128)(2,1)S(1)}, bf16[2,512,256]{2,1,0:T(8,128)(2,1)}, u32[]{:S(2)}, u32[]{:S(2)}) collective-permute-start(bf16[2,512,256]{2,1,0:T(8,128)(2,1)S(1)} %collective-permute-done.2), channel_id=1, source_target_pairs={{0,16},{16,32},{32,48},{48,64},{64,80},{80,96},{96,112},{1,17},{17... | collective-permute-start | bytes 1572872 | tf_op jit(solution)/shard_map/ppermute | solution.py:14
  124.3 22.6 %collective-permute-start.8 = (bf16[2,512,256]{2,1,0:T(8,128)(2,1)}, bf16[2,512,256]{2,1,0:T(8,128)(2,1)}, u32[]{:S(2)}, u32[]{:S(2)}) collective-permute-start(bf16[2,512,256]{2,1,0:T(8,128)(2,1)} %collective-permute-done.7), channel_id=1, source_target_pairs={{0,16},{16,32},{32,48},{48,64},{64,80},{80,96},{96,112},{1,17},{17... | collective-permute-start | bytes 1572872 | tf_op jit(solution)/shard_map/ppermute | solution.py:14
  135.6 679.7 %collective-permute-start.4 = (bf16[2,512,256]{2,1,0:T(8,128)(2,1)}, bf16[2,512,256]{2,1,0:T(8,128)(2,1)}, u32[]{:S(2)}, u32[]{:S(2)}) collective-permute-start(bf16[2,512,256]{2,1,0:T(8,128)(2,1)} %collective-permute-done.3), channel_id=1, source_target_pairs={{0,16},{16,32},{32,48},{48,64},{64,80},{80,96},{96,112},{1,17},{17... | collective-permute-start | bytes 1572872 | tf_op jit(solution)/shard_map/ppermute | solution.py:14
  146.9 674.4 %collective-permute-start.9 = (bf16[2,512,256]{2,1,0:T(8,128)(2,1)}, bf16[2,512,256]{2,1,0:T(8,128)(2,1)}, u32[]{:S(2)}, u32[]{:S(2)}) collective-permute-start(bf16[2,512,256]{2,1,0:T(8,128)(2,1)} %collective-permute-done.8), channel_id=1, source_target_pairs={{0,16},{16,32},{32,48},{48,64},{64,80},{80,96},{96,112},{1,17},{17... | collective-permute-start | bytes 1572872 | tf_op jit(solution)/shard_map/ppermute | solution.py:14
  183.3 19.9 %collective-permute-start.1 = (f32[512,256]{1,0:T(8,128)S(1)}, f32[512,256]{1,0:T(8,128)}, u32[]{:S(2)}, u32[]{:S(2)}) collective-permute-start(f32[512,256]{1,0:T(8,128)S(1)} %get-tuple-element.432), channel_id=1, source_target_pairs={{0,16},{16,32},{32,48},{48,64},{64,80},{80,96},{96,112},{1,17},{17... | collective-permute-start | bytes 1572872 | tf_op jit(solution)/shard_map/while/body/eval_jaxpr/ppermute | solution.py:14
  206.4 37.9 %collective-permute-start = (f32[256,512]{1,0:T(8,128)S(1)}, f32[256,512]{1,0:T(8,128)}, u32[]{:S(2)}, u32[]{:S(2)}) collective-permute-start(f32[256,512]{1,0:T(8,128)S(1)} %get-tuple-element.431), channel_id=1, source_target_pairs={{0,16},{16,32},{32,48},{48,64},{64,80},{80,96},{96,112},{1,17},{17... | collective-permute-start | bytes 1572872 | tf_op jit(solution)/shard_map/while/body/eval_jaxpr/ppermute | solution.py:14
  236.5 19.0 %collective-permute-start.1 = (f32[512,256]{1,0:T(8,128)S(1)}, f32[512,256]{1,0:T(8,128)}, u32[]{:S(2)}, u32[]{:S(2)}) collective-permute-start(f32[512,256]{1,0:T(8,128)S(1)} %get-tuple-element.432), channel_id=1, source_target_pairs={{0,16},{16,32},{32,48},{48,64},{64,80},{80,96},{96,112},{1,17},{17... | collective-permute-start | bytes 1572872 | tf_op jit(solution)/shard_map/while/body/eval_jaxpr/ppermute | solution.py:14
  258.7 35.1 %collective-permute-start = (f32[256,512]{1,0:T(8,128)S(1)}, f32[256,512]{1,0:T(8,128)}, u32[]{:S(2)}, u32[]{:S(2)}) collective-permute-start(f32[256,512]{1,0:T(8,128)S(1)} %get-tuple-element.431), channel_id=1, source_target_pairs={{0,16},{16,32},{32,48},{48,64},{64,80},{80,96},{96,112},{1,17},{17... | collective-permute-start | bytes 1572872 | tf_op jit(solution)/shard_map/while/body/eval_jaxpr/ppermute | solution.py:14
  265.2 33.6 %collective-permute-start.1 = (f32[512,256]{1,0:T(8,128)S(1)}, f32[512,256]{1,0:T(8,128)}, u32[]{:S(2)}, u32[]{:S(2)}) collective-permute-start(f32[512,256]{1,0:T(8,128)S(1)} %get-tuple-element.432), channel_id=1, source_target_pairs={{0,16},{16,32},{32,48},{48,64},{64,80},{80,96},{96,112},{1,17},{17... | collective-permute-start | bytes 1572872 | tf_op jit(solution)/shard_map/while/body/eval_jaxpr/ppermute | solution.py:14
  301.9 20.8 %collective-permute-start = (f32[256,512]{1,0:T(8,128)S(1)}, f32[256,512]{1,0:T(8,128)}, u32[]{:S(2)}, u32[]{:S(2)}) collective-permute-start(f32[256,512]{1,0:T(8,128)S(1)} %get-tuple-element.431), channel_id=1, source_target_pairs={{0,16},{16,32},{32,48},{48,64},{64,80},{80,96},{96,112},{1,17},{17... | collective-permute-start | bytes 1572872 | tf_op jit(solution)/shard_map/while/body/eval_jaxpr/ppermute | solution.py:14
  335.0 34.3 %collective-permute-start = (f32[256,512]{1,0:T(8,128)S(1)}, f32[256,512]{1,0:T(8,128)}, u32[]{:S(2)}, u32[]{:S(2)}) collective-permute-start(f32[256,512]{1,0:T(8,128)S(1)} %get-tuple-element.431), channel_id=1, source_target_pairs={{0,16},{16,32},{32,48},{48,64},{64,80},{80,96},{96,112},{1,17},{17... | collective-permute-start | bytes 1572872 | tf_op jit(solution)/shard_map/while/body/eval_jaxpr/ppermute | solution.py:14
  375.9 35.4 %collective-permute-start = (f32[256,512]{1,0:T(8,128)S(1)}, f32[256,512]{1,0:T(8,128)}, u32[]{:S(2)}, u32[]{:S(2)}) collective-permute-start(f32[256,512]{1,0:T(8,128)S(1)} %get-tuple-element.431), channel_id=1, source_target_pairs={{0,16},{16,32},{32,48},{48,64},{64,80},{80,96},{96,112},{1,17},{17... | collective-permute-start | bytes 1572872 | tf_op jit(solution)/shard_map/while/body/eval_jaxpr/ppermute | solution.py:14
  388.1 26.5 %collective-permute-start.1 = (f32[512,256]{1,0:T(8,128)S(1)}, f32[512,256]{1,0:T(8,128)}, u32[]{:S(2)}, u32[]{:S(2)}) collective-permute-start(f32[512,256]{1,0:T(8,128)S(1)} %get-tuple-element.432), channel_id=1, source_target_pairs={{0,16},{16,32},{32,48},{48,64},{64,80},{80,96},{96,112},{1,17},{17... | collective-permute-start | bytes 1572872 | tf_op jit(solution)/shard_map/while/body/eval_jaxpr/ppermute | solution.py:14
  417.9 26.4 %collective-permute-start = (f32[256,512]{1,0:T(8,128)S(1)}, f32[256,512]{1,0:T(8,128)}, u32[]{:S(2)}, u32[]{:S(2)}) collective-permute-start(f32[256,512]{1,0:T(8,128)S(1)} %get-tuple-element.431), channel_id=1, source_target_pairs={{0,16},{16,32},{32,48},{48,64},{64,80},{80,96},{96,112},{1,17},{17... | collective-permute-start | bytes 1572872 | tf_op jit(solution)/shard_map/while/body/eval_jaxpr/ppermute | solution.py:14
  430.5 17.7 %collective-permute-start.1 = (f32[512,256]{1,0:T(8,128)S(1)}, f32[512,256]{1,0:T(8,128)}, u32[]{:S(2)}, u32[]{:S(2)}) collective-permute-start(f32[512,256]{1,0:T(8,128)S(1)} %get-tuple-element.432), channel_id=1, source_target_pairs={{0,16},{16,32},{32,48},{48,64},{64,80},{80,96},{96,112},{1,17},{17... | collective-permute-start | bytes 1572872 | tf_op jit(solution)/shard_map/while/body/eval_jaxpr/ppermute | solution.py:14
  451.4 34.0 %collective-permute-start = (f32[256,512]{1,0:T(8,128)S(1)}, f32[256,512]{1,0:T(8,128)}, u32[]{:S(2)}, u32[]{:S(2)}) collective-permute-start(f32[256,512]{1,0:T(8,128)S(1)} %get-tuple-element.431), channel_id=1, source_target_pairs={{0,16},{16,32},{32,48},{48,64},{64,80},{80,96},{96,112},{1,17},{17... | collective-permute-start | bytes 1572872 | tf_op jit(solution)/shard_map/while/body/eval_jaxpr/ppermute | solution.py:14
  471.0 18.9 %collective-permute-start.1 = (f32[512,256]{1,0:T(8,128)S(1)}, f32[512,256]{1,0:T(8,128)}, u32[]{:S(2)}, u32[]{:S(2)}) collective-permute-start(f32[512,256]{1,0:T(8,128)S(1)} %get-tuple-element.432), channel_id=1, source_target_pairs={{0,16},{16,32},{32,48},{48,64},{64,80},{80,96},{96,112},{1,17},{17... | collective-permute-start | bytes 1572872 | tf_op jit(solution)/shard_map/while/body/eval_jaxpr/ppermute | solution.py:14
  537.8 38.4 %collective-permute-start = (f32[256,512]{1,0:T(8,128)S(1)}, f32[256,512]{1,0:T(8,128)}, u32[]{:S(2)}, u32[]{:S(2)}) collective-permute-start(f32[256,512]{1,0:T(8,128)S(1)} %get-tuple-element.431), channel_id=1, source_target_pairs={{0,16},{16,32},{32,48},{48,64},{64,80},{80,96},{96,112},{1,17},{17... | collective-permute-start | bytes 1572872 | tf_op jit(solution)/shard_map/while/body/eval_jaxpr/ppermute | solution.py:14
  589.7 35.2 %collective-permute-start = (f32[256,512]{1,0:T(8,128)S(1)}, f32[256,512]{1,0:T(8,128)}, u32[]{:S(2)}, u32[]{:S(2)}) collective-permute-start(f32[256,512]{1,0:T(8,128)S(1)} %get-tuple-element.431), channel_id=1, source_target_pairs={{0,16},{16,32},{32,48},{48,64},{64,80},{80,96},{96,112},{1,17},{17... | collective-permute-start | bytes 1572872 | tf_op jit(solution)/shard_map/while/body/eval_jaxpr/ppermute | solution.py:14
  596.2 32.1 %collective-permute-start.1 = (f32[512,256]{1,0:T(8,128)S(1)}, f32[512,256]{1,0:T(8,128)}, u32[]{:S(2)}, u32[]{:S(2)}) collective-permute-start(f32[512,256]{1,0:T(8,128)S(1)} %get-tuple-element.432), channel_id=1, source_target_pairs={{0,16},{16,32},{32,48},{48,64},{64,80},{80,96},{96,112},{1,17},{17... | collective-permute-start | bytes 1572872 | tf_op jit(solution)/shard_map/while/body/eval_jaxpr/ppermute | solution.py:14
  631.5 19.0 %collective-permute-start = (f32[256,512]{1,0:T(8,128)S(1)}, f32[256,512]{1,0:T(8,128)}, u32[]{:S(2)}, u32[]{:S(2)}) collective-permute-start(f32[256,512]{1,0:T(8,128)S(1)} %get-tuple-element.431), channel_id=1, source_target_pairs={{0,16},{16,32},{32,48},{48,64},{64,80},{80,96},{96,112},{1,17},{17... | collective-permute-start | bytes 1572872 | tf_op jit(solution)/shard_map/while/body/eval_jaxpr/ppermute | solution.py:14
  661.3 32.5 %collective-permute-start = (f32[256,512]{1,0:T(8,128)S(1)}, f32[256,512]{1,0:T(8,128)}, u32[]{:S(2)}, u32[]{:S(2)}) collective-permute-start(f32[256,512]{1,0:T(8,128)S(1)} %get-tuple-element.431), channel_id=1, source_target_pairs={{0,16},{16,32},{32,48},{48,64},{64,80},{80,96},{96,112},{1,17},{17... | collective-permute-start | bytes 1572872 | tf_op jit(solution)/shard_map/while/body/eval_jaxpr/ppermute | solution.py:14
  682.8 20.0 %collective-permute-start.1 = (f32[512,256]{1,0:T(8,128)S(1)}, f32[512,256]{1,0:T(8,128)}, u32[]{:S(2)}, u32[]{:S(2)}) collective-permute-start(f32[512,256]{1,0:T(8,128)S(1)} %get-tuple-element.432), channel_id=1, source_target_pairs={{0,16},{16,32},{32,48},{48,64},{64,80},{80,96},{96,112},{1,17},{17... | collective-permute-start | bytes 1572872 | tf_op jit(solution)/shard_map/while/body/eval_jaxpr/ppermute | solution.py:14
  706.0 29.5 %collective-permute-start = (f32[256,512]{1,0:T(8,128)S(1)}, f32[256,512]{1,0:T(8,128)}, u32[]{:S(2)}, u32[]{:S(2)}) collective-permute-start(f32[256,512]{1,0:T(8,128)S(1)} %get-tuple-element.431), channel_id=1, source_target_pairs={{0,16},{16,32},{32,48},{48,64},{64,80},{80,96},{96,112},{1,17},{17... | collective-permute-start | bytes 1572872 | tf_op jit(solution)/shard_map/while/body/eval_jaxpr/ppermute | solution.py:14
  712.5 26.4 %collective-permute-start.1 = (f32[512,256]{1,0:T(8,128)S(1)}, f32[512,256]{1,0:T(8,128)}, u32[]{:S(2)}, u32[]{:S(2)}) collective-permute-start(f32[512,256]{1,0:T(8,128)S(1)} %get-tuple-element.432), channel_id=1, source_target_pairs={{0,16},{16,32},{32,48},{48,64},{64,80},{80,96},{96,112},{1,17},{17... | collective-permute-start | bytes 1572872 | tf_op jit(solution)/shard_map/while/body/eval_jaxpr/ppermute | solution.py:14
  742.1 22.3 %collective-permute-start = (f32[256,512]{1,0:T(8,128)S(1)}, f32[256,512]{1,0:T(8,128)}, u32[]{:S(2)}, u32[]{:S(2)}) collective-permute-start(f32[256,512]{1,0:T(8,128)S(1)} %get-tuple-element.431), channel_id=1, source_target_pairs={{0,16},{16,32},{32,48},{48,64},{64,80},{80,96},{96,112},{1,17},{17... | collective-permute-start | bytes 1572872 | tf_op jit(solution)/shard_map/while/body/eval_jaxpr/ppermute | solution.py:14
  775.7 29.3 %collective-permute-start = (f32[256,512]{1,0:T(8,128)S(1)}, f32[256,512]{1,0:T(8,128)}, u32[]{:S(2)}, u32[]{:S(2)}) collective-permute-start(f32[256,512]{1,0:T(8,128)S(1)} %get-tuple-element.431), channel_id=1, source_target_pairs={{0,16},{16,32},{32,48},{48,64},{64,80},{80,96},{96,112},{1,17},{17... | collective-permute-start | bytes 1572872 | tf_op jit(solution)/shard_map/while/body/eval_jaxpr/ppermute | solution.py:14
  792.1 21.6 %collective-permute-start.1 = (f32[512,256]{1,0:T(8,128)S(1)}, f32[512,256]{1,0:T(8,128)}, u32[]{:S(2)}, u32[]{:S(2)}) collective-permute-start(f32[512,256]{1,0:T(8,128)S(1)} %get-tuple-element.432), channel_id=1, source_target_pairs={{0,16},{16,32},{32,48},{48,64},{64,80},{80,96},{96,112},{1,17},{17... | collective-permute-start | bytes 1572872 | tf_op jit(solution)/shard_map/while/body/eval_jaxpr/ppermute | solution.py:14
  (24 other events, 1144.2 us)
Sparse Core Ops, SparseCore 0:
  9.0 62.6 all-gather.1
  853.4 158.8 reduce-scatter.1
where the time goes:
time: 1020 us
  starting transfers between devices  455 us (45%)
  waiting for transfers between devices  366 us (36%)
  matrix products  81.7 us (8%)
  other arithmetic  72.6 us (7%)
  local copies, waits for them, and re-layouts  25.6 us (3%)
  between operations  14.3 us (1%)
    ppermute x40, starting transfers between devices, shifted(): return lax.ppermute(block, axis, route)  455 us
    reduce_scatter x1, waiting for transfers between devices, body(): lax.psum_scatter(partial_value.astype(jnp.bfloat16), 'head', scatter_dime...  159 us
    ppermute x40, waiting for transfers between devices, shifted(): return lax.ppermute(block, axis, route)  142 us
    all_gather x1, waiting for transfers between devices, body(): piece = lax.all_gather(flattened, 'head', axis=1, tiled=True)  64.4 us
    select_n x16, other arithmetic, turn(): fast_all = jnp.where(live, stored, fast_all)  30.8 us
  transfers between devices with their start and end apart: 42, of which 27 were waited for; matrix products, arithmetic and copies ran while one was open for 14% of the time, Pallas kernels for 0%

commit v1 on v0

--- a/solution.py
+++ b/solution.py
@@ -106,7 +106,9 @@
         lookup_mapping_tensor.shape[0], lookup_mapping_tensor.shape[2]
     )
     head_dim = weights_in.shape[1] // 3
-    piece = lax.all_gather(flattened, "head", axis=1, tiled=True)
+    piece = jnp.concatenate(
+        lax.all_to_all(jnp.stack([flattened] * lax.axis_size("head")), "head", 0, 0), axis=1
+    )
     projected = jnp.dot(piece, weights_in, preferred_element_type=jnp.float32)
     rate_col = jnp.dot(piece, stepsize_mapping_matrix, preferred_element_type=jnp.float32)
     query_rows, keys, values, weighted = prepare(projected, rate_col, seqs)

time: 1020 us -> 1060 us (1.039)
  blocking collectives: 0 us -> 99 us
  waiting for transfers between devices: 366 us -> 311 us
  local copies, waits for them, and re-layouts: 25.6 us -> 39.8 us
  starting transfers between devices: 455 us -> 441 us
    all_to_all x0 -> x1, blocking collectives: none -> 99 us  [body(): lax.all_to_all(jnp.stack([flattened] * lax.axis_size('head')), 'head', 0, 0)]
    all_gather x1 -> x0, waiting for transfers between devices: 64.4 us -> none  [body(): piece = lax.all_gather(flattened, 'head', axis=1, tiled=True)]
    ppermute x40, starting transfers between devices: 455 us -> 441 us  [shifted(): return lax.ppermute(block, axis, route)]
    cond x4 -> x22, local copies, waits for them, and re-layouts: 0.01 us -> 11.3 us
  transfers between devices with their start and end apart: 42 -> 41, of which waited for: 27 -> 27; matrix products, arithmetic and copies ran while one was open for 14% -> 14% of each run, Pallas kernels for 0% -> 0%
where the time goes in v1:
time: 1060 us
  starting transfers between devices  441 us (42%)
  waiting for transfers between devices  311 us (29%)
  blocking collectives  99 us (9%)
  matrix products  77.3 us (7%)
  other arithmetic  72.6 us (7%)
  local copies, waits for them, and re-layouts  39.8 us (4%)
  between operations  14.3 us (1%)
    ppermute x40, starting transfers between devices, shifted(): return lax.ppermute(block, axis, route)  441 us
    reduce_scatter x1, waiting for transfers between devices, body(): lax.psum_scatter(partial_value.astype(jnp.bfloat16), 'head', scatter_dime...  166 us
    ppermute x40, waiting for transfers between devices, shifted(): return lax.ppermute(block, axis, route)  145 us
    all_to_all x1, blocking collectives, body(): lax.all_to_all(jnp.stack([flattened] * lax.axis_size('head')), 'head', 0, 0)  99 us
    select_n x16, other arithmetic, turn(): fast_all = jnp.where(live, stored, fast_all)  30.9 us
  transfers between devices with their start and end apart: 41, of which 27 were waited for; matrix products, arithmetic and copies ran while one was open for 14% of the time, Pallas kernels for 0%

profile of v1, /device:TPU:5, one launch (start us, length us, event | category | flops | bytes accessed | tf_op | source)
XLA Modules:
  0.0 1058.9 jit_solution(14762903156389281950)
XLA Ops:
  9.0 99.0 %all_to_all.5 = bf16[16,1024,256]{1,2,0:T(8,128)(2,1)S(1)} all-to-all(bf16[16,1024,256]{1,2,0:T(8,128)(2,1)S(1)} %stack.3), channel_id=1, replica_groups=mesh['seq'=8,'head'=16] {'head'}, dimensions={0} | all-to-all | bytes 16777216 | tf_op jit(solution)/shard_map/all_to_all | solution.py:110
  187.6 660.8 %while.19 = (s32[]{:T(128)}, f32[256,512]{1,0:T(8,128)S(1)}, f32[512,256]{1,0:T(8,128)}, f32[2,512,256]{2,1,0:T(8,128)}, s32[]{:T(128)}, /*index=5*/pred[]{:T(51...) while((s32[]{:T(128)}, f32[256,512]{1,0:T(8,128)S(1)}, ...), condition=%wide.region_9.10_spmd, body=%wide.region_4.9_spmd.sunk | while | flops 5647237120 | bytes 36965468 | solution.py:161
  189.8 26.2 %conditional.2 = (f32[256,512]{1,0:T(8,128)S(1)}, f32[512,256]{1,0:T(8,128)}, f32[1,512,256]{2,1,0:T(8,128)}) conditional(s32[]{:T(128)} %convert_element_type.110, (f32[256,512]{1,0:T(8,128)S(1)}, f32[512,256]{1,0:T(8,128)S(1)}) %tuple.60, (bf16[2,512,256]{2,1,0:T(8,128)(2,1)}, s32[]{:T(128)}, bf16[2,512,256]{2,1,0:T(8,128)(2,1)}, ...), branch_computations={%region_5.5_spmd, %region_6.8_spmd} | conditional | flops 5646843904 | bytes 28051604 | solution.py:153
  226.2 11.3 %collective-permute-done.1 = f32[512,256]{1,0:T(8,128)} collective-permute-done((f32[512,256]{1,0:T(8,128)}, f32[512,256]{1,0:T(8,128)}, u32[]{:S(2)}, u32[]{:S(2)}) %collective-permute-start.1) | collective-permute-done | bytes 524320 | tf_op jit(solution)/shard_map/while/body/eval_jaxpr/ppermute | solution.py:14
  241.4 29.1 %collective-permute-start = (f32[256,512]{1,0:T(8,128)S(1)}, f32[256,512]{1,0:T(8,128)S(1)}, u32[]{:S(2)}, u32[]{:S(2)}) collective-permute-start(f32[256,512]{1,0:T(8,128)S(1)} %get-tuple-element.431), channel_id=1, source_target_pairs={{0,16},{16,32},{32,48},{48,64},{64,80},{80,96},{96,112},{1,17},{17... | collective-permute-start | bytes 1572872 | tf_op jit(solution)/shard_map/while/body/eval_jaxpr/ppermute | solution.py:14
  278.6 11.3 %collective-permute-done.1 = f32[512,256]{1,0:T(8,128)} collective-permute-done((f32[512,256]{1,0:T(8,128)}, f32[512,256]{1,0:T(8,128)}, u32[]{:S(2)}, u32[]{:S(2)}) %collective-permute-start.1) | collective-permute-done | bytes 524320 | tf_op jit(solution)/shard_map/while/body/eval_jaxpr/ppermute | solution.py:14
  298.4 28.4 %collective-permute-start.1 = (f32[512,256]{1,0:T(8,128)}, f32[512,256]{1,0:T(8,128)}, u32[]{:S(2)}, u32[]{:S(2)}) collective-permute-start(f32[512,256]{1,0:T(8,128)} %get-tuple-element.432), channel_id=1, source_target_pairs={{0,16},{16,32},{32,48},{48,64},{64,80},{80,96},{96,112},{1,17},{17... | collective-permute-start | bytes 1572872 | tf_op jit(solution)/shard_map/while/body/eval_jaxpr/ppermute | solution.py:14
  337.3 10.3 collective-permute-start
  356.8 9.4 collective-permute-done.1
  370.0 19.5 %collective-permute-start = (f32[256,512]{1,0:T(8,128)S(1)}, f32[256,512]{1,0:T(8,128)S(1)}, u32[]{:S(2)}, u32[]{:S(2)}) collective-permute-start(f32[256,512]{1,0:T(8,128)S(1)} %get-tuple-element.431), channel_id=1, source_target_pairs={{0,16},{16,32},{32,48},{48,64},{64,80},{80,96},{96,112},{1,17},{17... | collective-permute-start | bytes 1572872 | tf_op jit(solution)/shard_map/while/body/eval_jaxpr/ppermute | solution.py:14
  389.5 12.1 %collective-permute-start.1 = (f32[512,256]{1,0:T(8,128)}, f32[512,256]{1,0:T(8,128)}, u32[]{:S(2)}, u32[]{:S(2)}) collective-permute-start(f32[512,256]{1,0:T(8,128)} %get-tuple-element.432), channel_id=1, source_target_pairs={{0,16},{16,32},{32,48},{48,64},{64,80},{80,96},{96,112},{1,17},{17... | collective-permute-start | bytes 1572872 | tf_op jit(solution)/shard_map/while/body/eval_jaxpr/ppermute | solution.py:14
  411.4 9.9 collective-permute-start
  421.3 22.8 %collective-permute-start.1 = (f32[512,256]{1,0:T(8,128)}, f32[512,256]{1,0:T(8,128)}, u32[]{:S(2)}, u32[]{:S(2)}) collective-permute-start(f32[512,256]{1,0:T(8,128)} %get-tuple-element.432), channel_id=1, source_target_pairs={{0,16},{16,32},{32,48},{48,64},{64,80},{80,96},{96,112},{1,17},{17... | collective-permute-start | bytes 1572872 | tf_op jit(solution)/shard_map/while/body/eval_jaxpr/ppermute | solution.py:14
  453.6 11.1 %collective-permute-start = (f32[256,512]{1,0:T(8,128)S(1)}, f32[256,512]{1,0:T(8,128)S(1)}, u32[]{:S(2)}, u32[]{:S(2)}) collective-permute-start(f32[256,512]{1,0:T(8,128)S(1)} %get-tuple-element.431), channel_id=1, source_target_pairs={{0,16},{16,32},{32,48},{48,64},{64,80},{80,96},{96,112},{1,17},{17... | collective-permute-start | bytes 1572872 | tf_op jit(solution)/shard_map/while/body/eval_jaxpr/ppermute | solution.py:14
  464.7 11.7 %collective-permute-start.1 = (f32[512,256]{1,0:T(8,128)}, f32[512,256]{1,0:T(8,128)}, u32[]{:S(2)}, u32[]{:S(2)}) collective-permute-start(f32[512,256]{1,0:T(8,128)} %get-tuple-element.432), channel_id=1, source_target_pairs={{0,16},{16,32},{32,48},{48,64},{64,80},{80,96},{96,112},{1,17},{17... | collective-permute-start | bytes 1572872 | tf_op jit(solution)/shard_map/while/body/eval_jaxpr/ppermute | solution.py:14
  486.9 18.3 %collective-permute-start = (f32[256,512]{1,0:T(8,128)S(1)}, f32[256,512]{1,0:T(8,128)S(1)}, u32[]{:S(2)}, u32[]{:S(2)}) collective-permute-start(f32[256,512]{1,0:T(8,128)S(1)} %get-tuple-element.431), channel_id=1, source_target_pairs={{0,16},{16,32},{32,48},{48,64},{64,80},{80,96},{96,112},{1,17},{17... | collective-permute-start | bytes 1572872 | tf_op jit(solution)/shard_map/while/body/eval_jaxpr/ppermute | solution.py:14
  505.3 14.1 %collective-permute-start.1 = (f32[512,256]{1,0:T(8,128)}, f32[512,256]{1,0:T(8,128)}, u32[]{:S(2)}, u32[]{:S(2)}) collective-permute-start(f32[512,256]{1,0:T(8,128)} %get-tuple-element.432), channel_id=1, source_target_pairs={{0,16},{16,32},{32,48},{48,64},{64,80},{80,96},{96,112},{1,17},{17... | collective-permute-start | bytes 1572872 | tf_op jit(solution)/shard_map/while/body/eval_jaxpr/ppermute | solution.py:14
  527.8 26.2 %conditional.2 = (f32[256,512]{1,0:T(8,128)S(1)}, f32[512,256]{1,0:T(8,128)}, f32[1,512,256]{2,1,0:T(8,128)}) conditional(s32[]{:T(128)} %convert_element_type.110, (f32[256,512]{1,0:T(8,128)S(1)}, f32[512,256]{1,0:T(8,128)S(1)}) %tuple.60, (bf16[2,512,256]{2,1,0:T(8,128)(2,1)}, s32[]{:T(128)}, bf16[2,512,256]{2,1,0:T(8,128)(2,1)}, ...), branch_computations={%region_5.5_spmd, %region_6.8_spmd} | conditional | flops 5646843904 | bytes 28051604 | solution.py:153
  561.4 10.7 %collective-permute-done.1 = f32[512,256]{1,0:T(8,128)} collective-permute-done((f32[512,256]{1,0:T(8,128)}, f32[512,256]{1,0:T(8,128)}, u32[]{:S(2)}, u32[]{:S(2)}) %collective-permute-start.1) | collective-permute-done | bytes 524320 | tf_op jit(solution)/shard_map/while/body/eval_jaxpr/ppermute | solution.py:14
  575.9 30.7 %collective-permute-start = (f32[256,512]{1,0:T(8,128)S(1)}, f32[256,512]{1,0:T(8,128)S(1)}, u32[]{:S(2)}, u32[]{:S(2)}) collective-permute-start(f32[256,512]{1,0:T(8,128)S(1)} %get-tuple-element.431), channel_id=1, source_target_pairs={{0,16},{16,32},{32,48},{48,64},{64,80},{80,96},{96,112},{1,17},{17... | collective-permute-start | bytes 1572872 | tf_op jit(solution)/shard_map/while/body/eval_jaxpr/ppermute | solution.py:14
  612.7 10.4 collective-permute-done.1
  631.5 28.4 %collective-permute-start.1 = (f32[512,256]{1,0:T(8,128)}, f32[512,256]{1,0:T(8,128)}, u32[]{:S(2)}, u32[]{:S(2)}) collective-permute-start(f32[512,256]{1,0:T(8,128)} %get-tuple-element.432), channel_id=1, source_target_pairs={{0,16},{16,32},{32,48},{48,64},{64,80},{80,96},{96,112},{1,17},{17... | collective-permute-start | bytes 1572872 | tf_op jit(solution)/shard_map/while/body/eval_jaxpr/ppermute | solution.py:14
  669.4 8.3 collective-permute-start
  686.9 7.8 collective-permute-done.1
  698.5 20.8 %collective-permute-start = (f32[256,512]{1,0:T(8,128)S(1)}, f32[256,512]{1,0:T(8,128)S(1)}, u32[]{:S(2)}, u32[]{:S(2)}) collective-permute-start(f32[256,512]{1,0:T(8,128)S(1)} %get-tuple-element.431), channel_id=1, source_target_pairs={{0,16},{16,32},{32,48},{48,64},{64,80},{80,96},{96,112},{1,17},{17... | collective-permute-start | bytes 1572872 | tf_op jit(solution)/shard_map/while/body/eval_jaxpr/ppermute | solution.py:14
  719.3 9.4 collective-permute-start.1
  730.6 9.1 collective-permute-done.1
  748.1 23.1 %collective-permute-start.1 = (f32[512,256]{1,0:T(8,128)}, f32[512,256]{1,0:T(8,128)}, u32[]{:S(2)}, u32[]{:S(2)}) collective-permute-start(f32[512,256]{1,0:T(8,128)} %get-tuple-element.432), channel_id=1, source_target_pairs={{0,16},{16,32},{32,48},{48,64},{64,80},{80,96},{96,112},{1,17},{17... | collective-permute-start | bytes 1572872 | tf_op jit(solution)/shard_map/while/body/eval_jaxpr/ppermute | solution.py:14
  780.6 10.7 %collective-permute-start = (f32[256,512]{1,0:T(8,128)S(1)}, f32[256,512]{1,0:T(8,128)S(1)}, u32[]{:S(2)}, u32[]{:S(2)}) collective-permute-start(f32[256,512]{1,0:T(8,128)S(1)} %get-tuple-element.431), channel_id=1, source_target_pairs={{0,16},{16,32},{32,48},{48,64},{64,80},{80,96},{96,112},{1,17},{17... | collective-permute-start | bytes 1572872 | tf_op jit(solution)/shard_map/while/body/eval_jaxpr/ppermute | solution.py:14
  811.9 17.1 %collective-permute-start = (f32[256,512]{1,0:T(8,128)S(1)}, f32[256,512]{1,0:T(8,128)S(1)}, u32[]{:S(2)}, u32[]{:S(2)}) collective-permute-start(f32[256,512]{1,0:T(8,128)S(1)} %get-tuple-element.431), channel_id=1, source_target_pairs={{0,16},{16,32},{32,48},{48,64},{64,80},{80,96},{96,112},{1,17},{17... | collective-permute-start | bytes 1572872 | tf_op jit(solution)/shard_map/while/body/eval_jaxpr/ppermute | solution.py:14
  829.0 10.2 collective-permute-start.1
  886.0 166.1 %reduce-scatter.2.cloned.1.call-done = bf16[1024,256]{1,0:T(8,128)(2,1)} async-done(((bf16[1024,4096]{1,0:T(8,128)(2,1)}), bf16[1024,256]{1,0:T(8,128)(2,1)}) %reduce-scatter.2.cloned.1.call-update) | async-done | bytes 524304 | tf_op jit(solution)/shard_map/reduce_scatter | solution.py:166
  (236 shorter events, 383.3 us)
Async XLA Ops:
  6.5 1045.5 %reduce-scatter.2.cloned.1.call-start = ((), (), s32[]{:S(2)}) async-start(), calls=%async_computation.2 | async-start | bytes 8912896 | tf_op jit(solution)/shard_map/reduce_scatter | solution.py:166
  124.9 21.4 %collective-permute-start.6 = (bf16[2,512,256]{2,1,0:T(8,128)(2,1)S(1)}, bf16[2,512,256]{2,1,0:T(8,128)(2,1)}, u32[]{:S(2)}, u32[]{:S(2)}) collective-permute-start(bf16[2,512,256]{2,1,0:T(8,128)(2,1)S(1)} %bitcast.75), channel_id=1, source_target_pairs={{0,16},{16,32},{32,48},{48,64},{64,80},{80,96},{96,112},{1,17},{17... | collective-permute-start | bytes 1572872 | tf_op jit(solution)/shard_map/ppermute | solution.py:14
  135.1 22.5 %collective-permute-start.3 = (bf16[2,512,256]{2,1,0:T(8,128)(2,1)}, bf16[2,512,256]{2,1,0:T(8,128)(2,1)}, u32[]{:S(2)}, u32[]{:S(2)}) collective-permute-start(bf16[2,512,256]{2,1,0:T(8,128)(2,1)} %collective-permute-done.2), channel_id=1, source_target_pairs={{0,16},{16,32},{32,48},{48,64},{64,80},{80,96},{96,112},{1,17},{17... | collective-permute-start | bytes 1572872 | tf_op jit(solution)/shard_map/ppermute | solution.py:14
  146.3 22.6 %collective-permute-start.7 = (bf16[2,512,256]{2,1,0:T(8,128)(2,1)}, bf16[2,512,256]{2,1,0:T(8,128)(2,1)}, u32[]{:S(2)}, u32[]{:S(2)}) collective-permute-start(bf16[2,512,256]{2,1,0:T(8,128)(2,1)} %collective-permute-done.6), channel_id=1, source_target_pairs={{0,16},{16,32},{32,48},{48,64},{64,80},{80,96},{96,112},{1,17},{17... | collective-permute-start | bytes 1572872 | tf_op jit(solution)/shard_map/ppermute | solution.py:14
  157.6 22.5 %collective-permute-start.4 = (bf16[2,512,256]{2,1,0:T(8,128)(2,1)}, bf16[2,512,256]{2,1,0:T(8,128)(2,1)}, u32[]{:S(2)}, u32[]{:S(2)}) collective-permute-start(bf16[2,512,256]{2,1,0:T(8,128)(2,1)} %collective-permute-done.3), channel_id=1, source_target_pairs={{0,16},{16,32},{32,48},{48,64},{64,80},{80,96},{96,112},{1,17},{17... | collective-permute-start | bytes 1572872 | tf_op jit(solution)/shard_map/ppermute | solution.py:14
  168.8 681.0 %collective-permute-start.8 = (bf16[2,512,256]{2,1,0:T(8,128)(2,1)}, bf16[2,512,256]{2,1,0:T(8,128)(2,1)}, u32[]{:S(2)}, u32[]{:S(2)}) collective-permute-start(bf16[2,512,256]{2,1,0:T(8,128)(2,1)} %collective-permute-done.7), channel_id=1, source_target_pairs={{0,16},{16,32},{32,48},{48,64},{64,80},{80,96},{96,112},{1,17},{17... | collective-permute-start | bytes 1572872 | tf_op jit(solution)/shard_map/ppermute | solution.py:14
  180.1 675.5 %collective-permute-start.5 = (bf16[2,512,256]{2,1,0:T(8,128)(2,1)}, bf16[2,512,256]{2,1,0:T(8,128)(2,1)}, u32[]{:S(2)}, u32[]{:S(2)}) collective-permute-start(bf16[2,512,256]{2,1,0:T(8,128)(2,1)} %collective-permute-done.4), channel_id=1, source_target_pairs={{0,16},{16,32},{32,48},{48,64},{64,80},{80,96},{96,112},{1,17},{17... | collective-permute-start | bytes 1572872 | tf_op jit(solution)/shard_map/ppermute | solution.py:14
  217.3 20.2 %collective-permute-start.1 = (f32[512,256]{1,0:T(8,128)}, f32[512,256]{1,0:T(8,128)}, u32[]{:S(2)}, u32[]{:S(2)}) collective-permute-start(f32[512,256]{1,0:T(8,128)} %get-tuple-element.432), channel_id=1, source_target_pairs={{0,16},{16,32},{32,48},{48,64},{64,80},{80,96},{96,112},{1,17},{17... | collective-permute-start | bytes 1572872 | tf_op jit(solution)/shard_map/while/body/eval_jaxpr/ppermute | solution.py:14
  241.4 37.1 %collective-permute-start = (f32[256,512]{1,0:T(8,128)S(1)}, f32[256,512]{1,0:T(8,128)S(1)}, u32[]{:S(2)}, u32[]{:S(2)}) collective-permute-start(f32[256,512]{1,0:T(8,128)S(1)} %get-tuple-element.431), channel_id=1, source_target_pairs={{0,16},{16,32},{32,48},{48,64},{64,80},{80,96},{96,112},{1,17},{17... | collective-permute-start | bytes 1572872 | tf_op jit(solution)/shard_map/while/body/eval_jaxpr/ppermute | solution.py:14
  270.6 19.3 %collective-permute-start.1 = (f32[512,256]{1,0:T(8,128)}, f32[512,256]{1,0:T(8,128)}, u32[]{:S(2)}, u32[]{:S(2)}) collective-permute-start(f32[512,256]{1,0:T(8,128)} %get-tuple-element.432), channel_id=1, source_target_pairs={{0,16},{16,32},{32,48},{48,64},{64,80},{80,96},{96,112},{1,17},{17... | collective-permute-start | bytes 1572872 | tf_op jit(solution)/shard_map/while/body/eval_jaxpr/ppermute | solution.py:14
  293.8 34.9 %collective-permute-start = (f32[256,512]{1,0:T(8,128)S(1)}, f32[256,512]{1,0:T(8,128)S(1)}, u32[]{:S(2)}, u32[]{:S(2)}) collective-permute-start(f32[256,512]{1,0:T(8,128)S(1)} %get-tuple-element.431), channel_id=1, source_target_pairs={{0,16},{16,32},{32,48},{48,64},{64,80},{80,96},{96,112},{1,17},{17... | collective-permute-start | bytes 1572872 | tf_op jit(solution)/shard_map/while/body/eval_jaxpr/ppermute | solution.py:14
  298.4 35.0 %collective-permute-start.1 = (f32[512,256]{1,0:T(8,128)}, f32[512,256]{1,0:T(8,128)}, u32[]{:S(2)}, u32[]{:S(2)}) collective-permute-start(f32[512,256]{1,0:T(8,128)} %get-tuple-element.432), channel_id=1, source_target_pairs={{0,16},{16,32},{32,48},{48,64},{64,80},{80,96},{96,112},{1,17},{17... | collective-permute-start | bytes 1572872 | tf_op jit(solution)/shard_map/while/body/eval_jaxpr/ppermute | solution.py:14
  337.3 19.5 %collective-permute-start = (f32[256,512]{1,0:T(8,128)S(1)}, f32[256,512]{1,0:T(8,128)S(1)}, u32[]{:S(2)}, u32[]{:S(2)}) collective-permute-start(f32[256,512]{1,0:T(8,128)S(1)} %get-tuple-element.431), channel_id=1, source_target_pairs={{0,16},{16,32},{32,48},{48,64},{64,80},{80,96},{96,112},{1,17},{17... | collective-permute-start | bytes 1572872 | tf_op jit(solution)/shard_map/while/body/eval_jaxpr/ppermute | solution.py:14
  347.6 18.6 %collective-permute-start.1 = (f32[512,256]{1,0:T(8,128)}, f32[512,256]{1,0:T(8,128)}, u32[]{:S(2)}, u32[]{:S(2)}) collective-permute-start(f32[512,256]{1,0:T(8,128)} %get-tuple-element.432), channel_id=1, source_target_pairs={{0,16},{16,32},{32,48},{48,64},{64,80},{80,96},{96,112},{1,17},{17... | collective-permute-start | bytes 1572872 | tf_op jit(solution)/shard_map/while/body/eval_jaxpr/ppermute | solution.py:14
  370.0 33.5 %collective-permute-start = (f32[256,512]{1,0:T(8,128)S(1)}, f32[256,512]{1,0:T(8,128)S(1)}, u32[]{:S(2)}, u32[]{:S(2)}) collective-permute-start(f32[256,512]{1,0:T(8,128)S(1)} %get-tuple-element.431), channel_id=1, source_target_pairs={{0,16},{16,32},{32,48},{48,64},{64,80},{80,96},{96,112},{1,17},{17... | collective-permute-start | bytes 1572872 | tf_op jit(solution)/shard_map/while/body/eval_jaxpr/ppermute | solution.py:14
  389.5 17.9 %collective-permute-start.1 = (f32[512,256]{1,0:T(8,128)}, f32[512,256]{1,0:T(8,128)}, u32[]{:S(2)}, u32[]{:S(2)}) collective-permute-start(f32[512,256]{1,0:T(8,128)} %get-tuple-element.432), channel_id=1, source_target_pairs={{0,16},{16,32},{32,48},{48,64},{64,80},{80,96},{96,112},{1,17},{17... | collective-permute-start | bytes 1572872 | tf_op jit(solution)/shard_map/while/body/eval_jaxpr/ppermute | solution.py:14
  411.4 34.7 %collective-permute-start = (f32[256,512]{1,0:T(8,128)S(1)}, f32[256,512]{1,0:T(8,128)S(1)}, u32[]{:S(2)}, u32[]{:S(2)}) collective-permute-start(f32[256,512]{1,0:T(8,128)S(1)} %get-tuple-element.431), channel_id=1, source_target_pairs={{0,16},{16,32},{32,48},{48,64},{64,80},{80,96},{96,112},{1,17},{17... | collective-permute-start | bytes 1572872 | tf_op jit(solution)/shard_map/while/body/eval_jaxpr/ppermute | solution.py:14
  421.3 28.5 %collective-permute-start.1 = (f32[512,256]{1,0:T(8,128)}, f32[512,256]{1,0:T(8,128)}, u32[]{:S(2)}, u32[]{:S(2)}) collective-permute-start(f32[512,256]{1,0:T(8,128)} %get-tuple-element.432), channel_id=1, source_target_pairs={{0,16},{16,32},{32,48},{48,64},{64,80},{80,96},{96,112},{1,17},{17... | collective-permute-start | bytes 1572872 | tf_op jit(solution)/shard_map/while/body/eval_jaxpr/ppermute | solution.py:14
  453.6 24.7 %collective-permute-start = (f32[256,512]{1,0:T(8,128)S(1)}, f32[256,512]{1,0:T(8,128)S(1)}, u32[]{:S(2)}, u32[]{:S(2)}) collective-permute-start(f32[256,512]{1,0:T(8,128)S(1)} %get-tuple-element.431), channel_id=1, source_target_pairs={{0,16},{16,32},{32,48},{48,64},{64,80},{80,96},{96,112},{1,17},{17... | collective-permute-start | bytes 1572872 | tf_op jit(solution)/shard_map/while/body/eval_jaxpr/ppermute | solution.py:14
  464.7 18.3 %collective-permute-start.1 = (f32[512,256]{1,0:T(8,128)}, f32[512,256]{1,0:T(8,128)}, u32[]{:S(2)}, u32[]{:S(2)}) collective-permute-start(f32[512,256]{1,0:T(8,128)} %get-tuple-element.432), channel_id=1, source_target_pairs={{0,16},{16,32},{32,48},{48,64},{64,80},{80,96},{96,112},{1,17},{17... | collective-permute-start | bytes 1572872 | tf_op jit(solution)/shard_map/while/body/eval_jaxpr/ppermute | solution.py:14
  486.9 34.3 %collective-permute-start = (f32[256,512]{1,0:T(8,128)S(1)}, f32[256,512]{1,0:T(8,128)S(1)}, u32[]{:S(2)}, u32[]{:S(2)}) collective-permute-start(f32[256,512]{1,0:T(8,128)S(1)} %get-tuple-element.431), channel_id=1, source_target_pairs={{0,16},{16,32},{32,48},{48,64},{64,80},{80,96},{96,112},{1,17},{17... | collective-permute-start | bytes 1572872 | tf_op jit(solution)/shard_map/while/body/eval_jaxpr/ppermute | solution.py:14
  505.3 20.3 %collective-permute-start.1 = (f32[512,256]{1,0:T(8,128)}, f32[512,256]{1,0:T(8,128)}, u32[]{:S(2)}, u32[]{:S(2)}) collective-permute-start(f32[512,256]{1,0:T(8,128)} %get-tuple-element.432), channel_id=1, source_target_pairs={{0,16},{16,32},{32,48},{48,64},{64,80},{80,96},{96,112},{1,17},{17... | collective-permute-start | bytes 1572872 | tf_op jit(solution)/shard_map/while/body/eval_jaxpr/ppermute | solution.py:14
  575.9 36.8 %collective-permute-start = (f32[256,512]{1,0:T(8,128)S(1)}, f32[256,512]{1,0:T(8,128)S(1)}, u32[]{:S(2)}, u32[]{:S(2)}) collective-permute-start(f32[256,512]{1,0:T(8,128)S(1)} %get-tuple-element.431), channel_id=1, source_target_pairs={{0,16},{16,32},{32,48},{48,64},{64,80},{80,96},{96,112},{1,17},{17... | collective-permute-start | bytes 1572872 | tf_op jit(solution)/shard_map/while/body/eval_jaxpr/ppermute | solution.py:14
  627.0 34.8 %collective-permute-start = (f32[256,512]{1,0:T(8,128)S(1)}, f32[256,512]{1,0:T(8,128)S(1)}, u32[]{:S(2)}, u32[]{:S(2)}) collective-permute-start(f32[256,512]{1,0:T(8,128)S(1)} %get-tuple-element.431), channel_id=1, source_target_pairs={{0,16},{16,32},{32,48},{48,64},{64,80},{80,96},{96,112},{1,17},{17... | collective-permute-start | bytes 1572872 | tf_op jit(solution)/shard_map/while/body/eval_jaxpr/ppermute | solution.py:14
  631.5 34.1 %collective-permute-start.1 = (f32[512,256]{1,0:T(8,128)}, f32[512,256]{1,0:T(8,128)}, u32[]{:S(2)}, u32[]{:S(2)}) collective-permute-start(f32[512,256]{1,0:T(8,128)} %get-tuple-element.432), channel_id=1, source_target_pairs={{0,16},{16,32},{32,48},{48,64},{64,80},{80,96},{96,112},{1,17},{17... | collective-permute-start | bytes 1572872 | tf_op jit(solution)/shard_map/while/body/eval_jaxpr/ppermute | solution.py:14
  698.5 32.1 %collective-permute-start = (f32[256,512]{1,0:T(8,128)S(1)}, f32[256,512]{1,0:T(8,128)S(1)}, u32[]{:S(2)}, u32[]{:S(2)}) collective-permute-start(f32[256,512]{1,0:T(8,128)S(1)} %get-tuple-element.431), channel_id=1, source_target_pairs={{0,16},{16,32},{32,48},{48,64},{64,80},{80,96},{96,112},{1,17},{17... | collective-permute-start | bytes 1572872 | tf_op jit(solution)/shard_map/while/body/eval_jaxpr/ppermute | solution.py:14
  719.3 20.4 %collective-permute-start.1 = (f32[512,256]{1,0:T(8,128)}, f32[512,256]{1,0:T(8,128)}, u32[]{:S(2)}, u32[]{:S(2)}) collective-permute-start(f32[512,256]{1,0:T(8,128)} %get-tuple-element.432), channel_id=1, source_target_pairs={{0,16},{16,32},{32,48},{48,64},{64,80},{80,96},{96,112},{1,17},{17... | collective-permute-start | bytes 1572872 | tf_op jit(solution)/shard_map/while/body/eval_jaxpr/ppermute | solution.py:14
  743.6 29.5 %collective-permute-start = (f32[256,512]{1,0:T(8,128)S(1)}, f32[256,512]{1,0:T(8,128)S(1)}, u32[]{:S(2)}, u32[]{:S(2)}) collective-permute-start(f32[256,512]{1,0:T(8,128)S(1)} %get-tuple-element.431), channel_id=1, source_target_pairs={{0,16},{16,32},{32,48},{48,64},{64,80},{80,96},{96,112},{1,17},{17... | collective-permute-start | bytes 1572872 | tf_op jit(solution)/shard_map/while/body/eval_jaxpr/ppermute | solution.py:14
  748.1 28.7 %collective-permute-start.1 = (f32[512,256]{1,0:T(8,128)}, f32[512,256]{1,0:T(8,128)}, u32[]{:S(2)}, u32[]{:S(2)}) collective-permute-start(f32[512,256]{1,0:T(8,128)} %get-tuple-element.432), channel_id=1, source_target_pairs={{0,16},{16,32},{32,48},{48,64},{64,80},{80,96},{96,112},{1,17},{17... | collective-permute-start | bytes 1572872 | tf_op jit(solution)/shard_map/while/body/eval_jaxpr/ppermute | solution.py:14
  780.6 19.8 %collective-permute-start = (f32[256,512]{1,0:T(8,128)S(1)}, f32[256,512]{1,0:T(8,128)S(1)}, u32[]{:S(2)}, u32[]{:S(2)}) collective-permute-start(f32[256,512]{1,0:T(8,128)S(1)} %get-tuple-element.431), channel_id=1, source_target_pairs={{0,16},{16,32},{32,48},{48,64},{64,80},{80,96},{96,112},{1,17},{17... | collective-permute-start | bytes 1572872 | tf_op jit(solution)/shard_map/while/body/eval_jaxpr/ppermute | solution.py:14
  811.9 29.3 %collective-permute-start = (f32[256,512]{1,0:T(8,128)S(1)}, f32[256,512]{1,0:T(8,128)S(1)}, u32[]{:S(2)}, u32[]{:S(2)}) collective-permute-start(f32[256,512]{1,0:T(8,128)S(1)} %get-tuple-element.431), channel_id=1, source_target_pairs={{0,16},{16,32},{32,48},{48,64},{64,80},{80,96},{96,112},{1,17},{17... | collective-permute-start | bytes 1572872 | tf_op jit(solution)/shard_map/while/body/eval_jaxpr/ppermute | solution.py:14
  829.0 19.3 %collective-permute-start.1 = (f32[512,256]{1,0:T(8,128)}, f32[512,256]{1,0:T(8,128)}, u32[]{:S(2)}, u32[]{:S(2)}) collective-permute-start(f32[512,256]{1,0:T(8,128)} %get-tuple-element.432), channel_id=1, source_target_pairs={{0,16},{16,32},{32,48},{48,64},{64,80},{80,96},{96,112},{1,17},{17... | collective-permute-start | bytes 1572872 | tf_op jit(solution)/shard_map/while/body/eval_jaxpr/ppermute | solution.py:14
  (23 other events, 1308.4 us)
Sparse Core Ops, SparseCore 0:
  886.1 165.9 reduce-scatter.1
